TPU v7x, 32 devices: a whole 2x2x4 slice. The times are simulated.
32 devices in a mesh: dp: 8 (over y, x, core), tensor: 4 (over z).
Axes of the slice: x: 2, y: 2, z: 4, core: 2. Of those that a mesh axis runs over, the one named last changes fastest.
Arguments:
- query: bfloat16 [8192, 5120], P('dp', 'tensor'), may hold values from -6 to 6
- keys: bfloat16 [8192, 1024], P('dp', 'tensor'), may hold values from -6 to 6
- values: bfloat16 [8192, 1024], P('dp', 'tensor'), may hold values from -6 to 6
- out_weight: bfloat16 [5120, 2560], P('tensor', 'dp'), may hold values from -0.078125 to 0.078125
- loss_grad: bfloat16 [8192, 2560], P('dp', 'tensor'), may hold values from -6 to 6
- lengths: int32 [8, 16], P('dp'), may hold values from 1 to 512, 1024 in all within a row
- languages: int32 [8, 16], P('dp'), may hold values from 0 to 28
- labels: int32 [8192], P('dp'), may hold values from -100 to 152063, as said below
Outputs:
- attention_result: bfloat16 [8192, 5120], P('dp', 'tensor')
- query_gradient: bfloat16 [8192, 5120], P('dp', 'tensor')
- key_gradient: bfloat16 [8192, 1024], P('dp', 'tensor')
- value_gradient: bfloat16 [8192, 1024], P('dp', 'tensor')
- projection_gradient: bfloat16 [5120, 2560], P('tensor')
Inputs may be any that keep to these rules, and one draw needn't show every extreme that they name: `labels`: each label is -100, meaning no loss on that token, or a token id below 152064.
All inputs are finite; a program needn't handle non-finite values.
Results may differ from a plain program's by a relative error of at most 0.02.
Values may be sent and summed in bfloat16 or wider, within the bound.
A program may use at most 192 MiB of HBM per device.

v0:
```python
import math

import jax
import jax.numpy as jnp
from jax import lax
from jax.sharding import PartitionSpec as P

QUERY_HEADS = 40
KEY_VALUE_HEADS = 8
HEAD_SIZE = 128
LANGS = 29
DOCS = 16


def token_docs(length_row, row_count):
    doc_ends = jnp.cumsum(length_row)
    places = jnp.arange(row_count, dtype=jnp.int32)
    return jnp.sum((places[:, None] >= doc_ends[None, :]).astype(jnp.int32), axis=1)


def masked_scores(query_rows, key_rows, allowed, factor):
    scores = (
        jnp.einsum("rgd,kd->grk", query_rows, key_rows, preferred_element_type=jnp.float32) * factor
    )
    return jnp.where(allowed[None], scores, -1e30)


def block_forward(query_rows, key_rows, value_rows, allowed, factor):
    scores = masked_scores(query_rows, key_rows, allowed, factor)
    row_top = jnp.max(scores, axis=2, keepdims=True)
    log_total = row_top + jnp.log(jnp.sum(jnp.exp(scores - row_top), axis=2, keepdims=True))
    weights = jnp.exp(scores - log_total).astype(jnp.bfloat16)
    result = jnp.einsum("grk,kd->rgd", weights, value_rows, preferred_element_type=jnp.float32)
    return (result.astype(jnp.bfloat16), log_total[:, :, 0])


def block_backward(
    query_rows, key_rows, value_rows, allowed, out_rows, log_rows, grad_rows, factor
):
    scores = masked_scores(query_rows, key_rows, allowed, factor)
    weights = jnp.exp(scores - log_rows[:, :, None])
    value_gradient = jnp.einsum(
        "grk,rgd->kd", weights.astype(jnp.bfloat16), grad_rows, preferred_element_type=jnp.float32
    )
    weight_grad = jnp.einsum(
        "rgd,kd->grk", grad_rows, value_rows, preferred_element_type=jnp.float32
    )
    diagonal_term = jnp.einsum(
        "rgd,rgd->gr", grad_rows, out_rows, preferred_element_type=jnp.float32
    )
    score_grad = (weights * (weight_grad - diagonal_term[:, :, None]) * factor).astype(jnp.bfloat16)
    query_gradient = jnp.einsum(
        "grk,kd->rgd", score_grad, key_rows, preferred_element_type=jnp.float32
    )
    key_gradient = jnp.einsum(
        "grk,rgd->kd", score_grad, query_rows, preferred_element_type=jnp.float32
    )
    return (query_gradient, key_gradient, value_gradient)


def pack_layout(doc_ids):
    row_count = doc_ids.shape[0]
    places = jnp.arange(row_count, dtype=jnp.int32)
    allowed = (doc_ids[:, None] == doc_ids[None, :]) & (places[:, None] >= places[None, :])
    half_rows = row_count // 2
    key_step = row_count // 8
    first_row = jnp.min(jnp.where(doc_ids == doc_ids[half_rows], places, row_count))
    return (allowed, half_rows, key_step, first_row // key_step)


def pack_forward(query, keys, values, doc_ids, factor):
    allowed, half_rows, key_step, bucket = pack_layout(doc_ids)
    row_count = doc_ids.shape[0]
    group_size = QUERY_HEADS // KEY_VALUE_HEADS
    outs = []
    logs = []
    for head_cluster in range(keys.shape[1] // HEAD_SIZE):
        query_part = query[
            :, head_cluster * group_size * HEAD_SIZE : (head_cluster + 1) * group_size * HEAD_SIZE
        ].reshape(row_count, group_size, HEAD_SIZE)
        key_part = keys[:, head_cluster * HEAD_SIZE : (head_cluster + 1) * HEAD_SIZE]
        value_part = values[:, head_cluster * HEAD_SIZE : (head_cluster + 1) * HEAD_SIZE]
        early_out, early_log = block_forward(
            query_part[:half_rows],
            key_part[:half_rows],
            value_part[:half_rows],
            allowed[:half_rows, :half_rows],
            factor,
        )

        def later_block(bucket_id):
            first_key = bucket_id * key_step

            def run_block(operands):
                query_late, key_all, value_all = operands
                return block_forward(
                    query_late,
                    key_all[first_key:],
                    value_all[first_key:],
                    allowed[half_rows:, first_key:],
                    factor,
                )

            return run_block

        late_out, late_log = lax.switch(
            bucket,
            [later_block(bucket_id) for bucket_id in range(5)],
            (query_part[half_rows:], key_part, value_part),
        )
        outs.append(
            jnp.concatenate([early_out, late_out], axis=0).reshape(
                row_count, group_size * HEAD_SIZE
            )
        )
        logs.append(jnp.concatenate([early_log, late_log], axis=1))
    return (jnp.concatenate(outs, axis=1), jnp.stack(logs, axis=0))


def pack_backward(query, keys, values, doc_ids, attn_rows, log_rows, grad_rows, factor):
    allowed, half_rows, key_step, bucket = pack_layout(doc_ids)
    row_count = doc_ids.shape[0]
    group_size = QUERY_HEADS // KEY_VALUE_HEADS
    query_parts = []
    key_parts = []
    value_parts = []
    for head_cluster in range(keys.shape[1] // HEAD_SIZE):
        span = slice(
            head_cluster * group_size * HEAD_SIZE, (head_cluster + 1) * group_size * HEAD_SIZE
        )
        query_part = query[:, span].reshape(row_count, group_size, HEAD_SIZE)
        attn_part = attn_rows[:, span].reshape(row_count, group_size, HEAD_SIZE)
        grad_part = grad_rows[:, span].reshape(row_count, group_size, HEAD_SIZE)
        key_part = keys[:, head_cluster * HEAD_SIZE : (head_cluster + 1) * HEAD_SIZE]
        value_part = values[:, head_cluster * HEAD_SIZE : (head_cluster + 1) * HEAD_SIZE]
        log_part = log_rows[head_cluster]
        early_query, early_key, early_value = block_backward(
            query_part[:half_rows],
            key_part[:half_rows],
            value_part[:half_rows],
            allowed[:half_rows, :half_rows],
            attn_part[:half_rows],
            log_part[:, :half_rows],
            grad_part[:half_rows],
            factor,
        )

        def later_block(bucket_id):
            first_key = bucket_id * key_step

            def run_block(operands):
                query_late, key_all, value_all, attn_late, log_late, grad_late = operands
                late_query, late_key, late_value = block_backward(
                    query_late,
                    key_all[first_key:],
                    value_all[first_key:],
                    allowed[half_rows:, first_key:],
                    attn_late,
                    log_late,
                    grad_late,
                    factor,
                )
                return (
                    late_query,
                    jnp.pad(late_key, ((first_key, 0), (0, 0))),
                    jnp.pad(late_value, ((first_key, 0), (0, 0))),
                )

            return run_block

        late_query, late_key, late_value = lax.switch(
            bucket,
            [later_block(bucket_id) for bucket_id in range(5)],
            (
                query_part[half_rows:],
                key_part,
                value_part,
                attn_part[half_rows:],
                log_part[:, half_rows:],
                grad_part[half_rows:],
            ),
        )
        tail_rows = row_count - half_rows
        key_total = late_key + jnp.pad(early_key, ((0, tail_rows), (0, 0)))
        value_total = late_value + jnp.pad(early_value, ((0, tail_rows), (0, 0)))
        query_parts.append(
            jnp.concatenate([early_query, late_query], axis=0)
            .astype(jnp.bfloat16)
            .reshape(row_count, group_size * HEAD_SIZE)
        )
        key_parts.append(key_total.astype(jnp.bfloat16))
        value_parts.append(value_total.astype(jnp.bfloat16))
    return (
        jnp.concatenate(query_parts, axis=1),
        jnp.concatenate(key_parts, axis=1),
        jnp.concatenate(value_parts, axis=1),
    )


def shards(query, keys, values, out_weight, loss_grad, lengths, languages, labels):
    factor = 1.0 / math.sqrt(HEAD_SIZE)
    row_count = query.shape[0]
    doc_ids = token_docs(lengths[0], row_count)
    attention_result, log_rows = pack_forward(query, keys, values, doc_ids, factor)
    token_lang = jnp.sum(
        jnp.where(
            doc_ids[:, None] == jnp.arange(DOCS, dtype=jnp.int32)[None, :], languages[0][None, :], 0
        ),
        axis=1,
    )
    counted = labels != -100
    lang_match = token_lang[:, None] == jnp.arange(LANGS, dtype=jnp.int32)[None, :]
    local_counts = jnp.sum((lang_match & counted[:, None]).astype(jnp.int32), axis=0)
    counts = lax.psum(local_counts, "dp").astype(jnp.float32)
    lang_weight = jnp.sqrt(jnp.sum(counts) / (LANGS * jnp.maximum(counts, 1.0)))
    token_weight = jnp.where(
        counted, jnp.sum(jnp.where(lang_match, lang_weight[None, :], 0.0), axis=1), 0.0
    )
    full_grad = lax.all_gather(loss_grad, "tensor", axis=1, tiled=True)
    weighted = (token_weight[:, None] * full_grad.astype(jnp.float32)).astype(jnp.bfloat16)
    out_grad = lax.dot_general(
        weighted,
        lax.all_gather(out_weight, "dp", axis=1, tiled=True),
        (((1,), (1,)), ((), ())),
        preferred_element_type=jnp.float32,
    ).astype(jnp.bfloat16)
    local_term = lax.dot_general(
        attention_result, weighted, (((0,), (0,)), ((), ())), preferred_element_type=jnp.float32
    )
    projection_gradient = lax.psum(local_term, "dp").astype(jnp.bfloat16)
    query_gradient, key_gradient, value_gradient = pack_backward(
        query, keys, values, doc_ids, attention_result, log_rows, out_grad, factor
    )
    return (attention_result, query_gradient, key_gradient, value_gradient, projection_gradient)


def solution(mesh):
    in_specs = (
        P("dp", "tensor"),
        P("dp", "tensor"),
        P("dp", "tensor"),
        P("tensor", "dp"),
        P("dp", "tensor"),
        P("dp", None),
        P("dp", None),
        P("dp"),
    )
    out_specs = (
        P("dp", "tensor"),
        P("dp", "tensor"),
        P("dp", "tensor"),
        P("dp", "tensor"),
        P("tensor", None),
    )
    return jax.shard_map(shards, mesh=mesh, in_specs=in_specs, out_specs=out_specs, check_vma=False)
```

profile of v0, /device:TPU:0, one launch (start us, length us, event | category | flops | bytes accessed | tf_op | source)
XLA Modules:
  0.0 605.3 jit_solution(3211204294735181624)
XLA Ops:
  14.7 3.4 fusion.356
  25.3 24.7 %conditional.9 = (f32[5,512]{1,0:T(8,128)}, bf16[512,5,128]{2,0,1:T(8,128)(2,1)}) conditional(s32[]{:T(128)} %clamp.2, (pred[1024,1024]{0,1:T(8,128)(4,1)S(1)}, bf16[1024,128]{1,0:T(8,128)(2,1)}, bf16[512,5,128]{0,2,1:T(8,128)(2,1)}, bf16[1024,128]{1,0:T(8,128)(2,1)}) %tuple.143, (pred[1024,1024]{0,1:T(8,128)(4,1)S(1)}, ...), branch_computations={%region_22.25_spmd, %region_25.28_spmd, %region_28.31_spmd, %regio... | conditional | flops 1371338240 | bytes 35985424
  32.9 2.4 fusion.92
  37.3 3.9 fusion.96
  50.1 16.5 %conditional.8 = (f32[5,512]{1,0:T(8,128)}, bf16[512,5,128]{2,0,1:T(8,128)(2,1)}) conditional(s32[]{:T(128)} %clamp.2, (pred[1024,1024]{0,1:T(8,128)(4,1)S(1)}, bf16[1024,128]{1,0:T(8,128)(2,1)S(1)}, bf16[512,5,128]{0,2,1:T(8,128)(2,1)S(1)}, bf16[1024,128]{1,0:T(8,128)(2,1)S(1)}) %tuple.288, ...), branch_computations={%region_5.8_spmd, %region_8.11_spmd, %region_11.14_spmd, %region_1... | conditional | flops 1371338240 | bytes 35985424
  62.7 3.6 fusion.38
  66.8 11.7 %psum.14 = s32[29]{0:T(128)S(1)} all-reduce(s32[29]{0:T(128)S(1)} %convert_reduce_fusion), channel_id=1, replica_groups=mesh['dp'=8,'tensor'=4] {'dp'}, use_global_device_ids=true, to_apply=%region_39.40 | all-reduce | flops 29 | bytes 232 | tf_op jit(solution)/shard_map/psum | solution.py:214
  82.5 3.3 exponential_reduce_fusion.11
  89.9 20.5 %all-gather.3.cloned.1.call-done = bf16[1024,2560]{1,0:T(8,128)(2,1)} async-done(((bf16[1024,640]{1,0:T(8,128)(2,1)}), bf16[1024,2560]{1,0:T(8,128)(2,1)}) %all-gather.3.cloned.1.call-update) | async-done | bytes 5242896 | tf_op jit(solution)/shard_map/all_gather | solution.py:219
  110.4 46.9 %all-gather.5.cloned.1.call-done = bf16[1280,2560]{0,1:T(8,128)(2,1)} async-done(((bf16[1280,320]{0,1:T(8,128)(2,1)}), bf16[1280,2560]{0,1:T(8,128)(2,1)}) %all-gather.5.cloned.1.call-update) | async-done | bytes 6553616 | tf_op jit(solution)/shard_map/all_gather | solution.py:223
  157.3 11.4 %convolution_convert_fusion.10 = bf16[1024,1280]{1,0:T(8,128)(2,1)S(1)} fusion(bf16[1280,2560]{0,1:T(8,128)(2,1)} %all-gather.5.cloned.1.call-done, bf16[1024,2560]{1,0:T(8,128)(2,1)} %all-gather.3.cloned.1.call-done, f32[1024]{0:T(1024)} %broadcast_select_fusion), kind=kOutput, calls=%fused_computation.399 | convolution fusion | flops 6720061440 | bytes 14422016 | tf_op jit(solution)/shard_map/dot_general | solution.py:221
  174.5 5.5 multiply_reduce_fusion.10
  180.0 4.8 convolution_bitcast_fusion.10
  184.7 4.6 fusion.322
  197.9 5.4 multiply_reduce_fusion.11
  203.4 4.7 convolution_bitcast_fusion.11
  208.1 4.6 fusion.325
  216.9 46.6 %conditional.11 = (f32[1024,128]{0,1:T(8,128)}, f32[1024,128]{0,1:T(8,128)}, bf16[512,640]{1,0:T(8,128)(2,1)}) conditional(s32[]{:T(128)} %clamp.2, (pred[1024,1024]{0,1:T(8,128)(4,1)S(1)}, bf16[1024,128]{1,0:T(8,128)(2,1)}, bf16[512,5,128]{0,2,1:T(8,128)(2,1)}, f32[5,512]{1,0:T(8,128)}, bf16[1024,128]{1,0:T(8,128)(2,1)}, ...), branch_computations={%region_47.48_spmd, %region_48.49_spmd, %region_49.50_spmd, %regio... | conditional | flops 3385587200 | bytes 70971472 | solution.py:171
  224.8 2.6 copy.322
  229.4 2.5 copy.463
  231.9 3.1 multiply_reduce_fusion.8
  238.3 3.4 fusion.287
  241.7 3.5 fusion.280
  245.2 3.0 convolution_bitcast_fusion.8
  248.2 2.5 convolution_convert_fusion.8
  263.5 41.9 %conditional.10 = (f32[1024,128]{0,1:T(8,128)S(1)}, f32[1024,128]{0,1:T(8,128)S(1)}, bf16[512,640]{1,0:T(8,128)(2,1)S(1)}) conditional(s32[]{:T(128)} %clamp.2, (pred[1024,1024]{0,1:T(8,128)(4,1)}, bf16[1024,128]{1,0:T(8,128)(2,1)S(1)}, bf16[512,5,128]{0,2,1:T(8,128)(2,1)S(1)}, f32[5,512]{1,0:T(8,128)}, ...), branch_computations={%region_42.43_spmd, %region_43.44_spmd, %region_44.45_spmd, %regio... | conditional | flops 3385587200 | bytes 72020072 | solution.py:171
  282.5 2.6 copy.299
  291.6 2.7 fusion.185
  294.3 3.3 fusion.178
  322.0 2.7 copy.337
  324.7 12.7 %fusion.331 = f32[1280,2560]{1,0:T(8,128)} fusion(bf16[1024,2560]{1,0:T(8,128)(2,1)} %all-gather.3.cloned.1.call-done, f32[1024]{0:T(1024)S(1)} %copy-done.51, bf16[1024,640]{0,1:T(8,128)(2,1)} %bitcast.875, bf16[1024,640]{0,1:T(8,128)(2,1)} %bitcast.877), kind=kOutput, calls=%fused_computation.404 | convolution fusion | flops 6723993600 | bytes 20975616 | tf_op jit(solution)/shard_map/dot_general | solution.py:227
  337.4 259.2 %all-reduce.21 = bf16[1280,2560]{1,0:T(8,128)(2,1)} all-reduce(f32[1280,2560]{1,0:T(8,128)} %fusion.331), channel_id=1, replica_groups=mesh['dp'=8,'tensor'=4] {'dp'}, use_global_device_ids=true, to_apply=%region_52.53 | all-reduce | flops 3276800 | bytes 19660800 | tf_op jit(solution)/shard_map/psum | solution.py:230
  (143 shorter events, 84.5 us)
Async XLA Ops:
  7.2 103.2 %all-gather.3.cloned.1.call-start = ((), (), s32[]{:S(2)}) async-start(), calls=%async_computation | async-start | bytes 6553600 | tf_op jit(solution)/shard_map/all_gather | solution.py:219
  7.9 149.4 %all-gather.5.cloned.1.call-start = ((), (), s32[]{:S(2)}) async-start(), calls=%async_computation.1 | async-start | bytes 7372800 | tf_op jit(solution)/shard_map/all_gather | solution.py:223
  14.6 35.4 %copy-start = (pred[1024,1024]{0,1:T(8,128)(4,1)}, pred[1024,1024]{0,1:T(8,128)(4,1)S(1)}, u32[]{:S(2)}) copy-start(pred[1024,1024]{0,1:T(8,128)(4,1)S(1)} %fusion.328) | copy-start | bytes 3145732
  14.7 71.2 %copy-start.24 = (pred[512,512]{0,1:T(8,128)(4,1)}, pred[512,512]{0,1:T(8,128)(4,1)S(1)}, u32[]{:S(2)}) copy-start(pred[512,512]{0,1:T(8,128)(4,1)S(1)} %slice.324) | copy-start | bytes 786436
  22.0 58.5 %copy-start.4 = (bf16[512,640]{0,1:T(8,128)(2,1)}, bf16[512,640]{0,1:T(8,128)(2,1)S(1)}, u32[]{:S(2)}) copy-start(bf16[512,640]{0,1:T(8,128)(2,1)S(1)} %copy.578) | copy-start | bytes 1966084
  25.3 24.8 %copy-start.43 = (bf16[1024,128]{1,0:T(8,128)(2,1)}, bf16[1024,128]{1,0:T(8,128)(2,1)S(1)}, u32[]{:S(2)}) copy-start(bf16[1024,128]{1,0:T(8,128)(2,1)S(1)} %get-tuple-element.734) | copy-start | bytes 786436
  50.1 16.5 %copy-start.52 = (s32[1,16]{1,0:T(1,128)S(1)}, s32[1,16]{1,0:T(1,128)}, u32[]{:S(2)}) copy-start(s32[1,16]{1,0:T(1,128)} %param.34) | copy-start | bytes 196
  50.1 16.6 %copy-start.49 = (s32[1024]{0:T(1024)S(1)}, s32[1024]{0:T(1024)}, u32[]{:S(2)}) copy-start(s32[1024]{0:T(1024)} %param.35) | copy-start | bytes 12292
  66.6 15.9 %copy-start.28 = (bf16[512,640]{0,1:T(8,128)(2,1)S(1)}, bf16[512,640]{0,1:T(8,128)(2,1)}, u32[]{:S(2)}) copy-start(bf16[512,640]{0,1:T(8,128)(2,1)} %copy.580) | copy-start | bytes 1966084
  82.5 3.4 copy-start.2
  85.8 2.4 copy-start.3
  174.5 5.5 copy-start.13
  174.5 5.5 copy-start.25
  174.5 5.5 copy-start.50
  184.7 4.6 copy-start.29
  197.9 5.5 copy-start.12
  197.9 5.5 copy-start.26
  208.1 4.6 copy-start.5
  212.7 4.2 copy-start.1
  236.1 2.3 copy-start.17
  236.1 2.3 copy-start.39
  290.4 1.2 copy-start.40
  291.6 2.7 copy-start.47
  305.4 6.7 %copy-start.8 = (bf16[512,640]{1,0:T(8,128)(2,1)}, bf16[512,640]{1,0:T(8,128)(2,1)S(1)}, u32[]{:S(2)}) copy-start(bf16[512,640]{1,0:T(8,128)(2,1)S(1)} %get-tuple-element.702) | copy-start | bytes 1966084
  306.4 5.8 copy-start.10
  309.3 6.6 %copy-start.11 = (bf16[5,512,128]{1,2,0:T(8,128)(2,1)S(1)}, bf16[5,512,128]{1,2,0:T(8,128)(2,1)}, u32[]{:S(2)}) copy-start(bf16[5,512,128]{1,2,0:T(8,128)(2,1)} %convolution_convert_fusion.12) | copy-start | bytes 1966084
  312.2 4.8 copy-start.30
  312.5 5.5 copy-start.32
  320.1 4.6 copy-start.51
  337.4 259.2 %copy-start.6 = (bf16[512,640]{1,0:T(8,128)(2,1)S(1)}, bf16[512,640]{1,0:T(8,128)(2,1)}, u32[]{:S(2)}) copy-start(bf16[512,640]{1,0:T(8,128)(2,1)} %copy.304) | copy-start | bytes 1966084
  337.4 259.2 %copy-start.7 = (bf16[512,640]{1,0:T(8,128)(2,1)S(1)}, bf16[512,640]{1,0:T(8,128)(2,1)}, u32[]{:S(2)}) copy-start(bf16[512,640]{1,0:T(8,128)(2,1)} %get-tuple-element.705) | copy-start | bytes 1966084
  337.4 259.2 %copy-start.9 = (bf16[512,640]{1,0:T(8,128)(2,1)S(1)}, bf16[512,640]{1,0:T(8,128)(2,1)}, u32[]{:S(2)}) copy-start(bf16[512,640]{1,0:T(8,128)(2,1)} %copy-done.8) | copy-start | bytes 1966084
  (3 other events, 2.9 us)
Sparse Core Ops, SparseCore 0:
  9.6 100.7 all-gather.2
  112.3 44.9 all-gather.4
where the time goes:
time: 612 us; the launch traced here: 605 us
  blocking collectives  271 us (44%)
  matrix products  102 us (17%)
  waiting for transfers between devices  68.8 us (11%)
  loops' own time  63.1 us (10%)
  local copies, waits for them, and re-layouts  57.8 us (9%)
  other arithmetic  25.8 us (4%)
  between operations  17.3 us (3%)
    psum x1, blocking collectives, shards(): projection_gradient = lax.psum(local_term, 'dp').astype(jnp.bfloat16)  259 us
    all_gather x1, waiting for transfers between devices, shards(): lax.all_gather(out_weight, 'dp', axis=1, tiled=True)  46.9 us
    another operation x2, loops' own time, pack_backward(): lax.switch(bucket, [later_block(bucket_id) for bucket_id in range(5)], (q...  37.1 us
    unnamed x2, loops' own time  26.1 us
    all_gather x1, waiting for transfers between devices, shards(): full_grad = lax.all_gather(loss_grad, 'tensor', axis=1, tiled=True)  20.5 us
    dot_general x4, matrix products, block_forward(): jnp.einsum('grk,kd->rgd', weights, value_rows, preferred_element_type=jnp...  18.4 us
    unnamed x65, local copies, waits for them, and re-layouts  17.9 us
    dot_general x4, matrix products, block_backward(): jnp.einsum('rgd,kd->grk', grad_rows, value_rows, preferred_element_type=j...  16 us
  transfers between devices with their start and end apart: 2, of which 2 were waited for; matrix products, arithmetic and copies ran while one was open for 6% of the time, Pallas kernels for 0%

commit v1 on v0

v1 whole, which is shorter than its diff:
```python
import math

import jax
import jax.numpy as jnp
from jax import lax
from jax.experimental import pallas as pl
from jax.experimental.pallas import tpu as pltpu
from jax.sharding import PartitionSpec as P

QUERY_HEADS = 40
KEY_VALUE_HEADS = 8
HEAD_SIZE = 128
LANGS = 29
DOCS = 16
GROUP = QUERY_HEADS // KEY_VALUE_HEADS
BLOCK = 256
REACH = 512
FACTOR = 1.0 / math.sqrt(HEAD_SIZE)
LOG2E = math.log2(math.e)
NT = (((1,), (1,)), ((), ()))
NN = (((1,), (0,)), ((), ()))
TN = (((0,), (0,)), ((), ()))


def dot(a, b, dims):
    return lax.dot_general(a, b, dims, preferred_element_type=jnp.float32)


def windows(rows):
    return [(at, max(0, at - REACH), at + BLOCK) for at in range(0, rows, BLOCK)]


def fill_bias(starts_ref, bias_ref, rows):
    for index, (at, low, high) in enumerate(windows(rows)):
        shape = (high - low, BLOCK)
        key_place = low + lax.broadcasted_iota(jnp.int32, shape, 0)
        query_place = at + lax.broadcasted_iota(jnp.int32, shape, 1)
        allowed = (key_place >= starts_ref[0:1, at : at + BLOCK]) & (key_place <= query_place)
        bias_ref[index, 0 : high - low, :] = jnp.where(allowed, 0.0, -1e30)


def forward_kernel(starts_ref, q_ref, k_ref, v_ref, out_ref, log_ref, bias_ref, vt_ref):
    rows = q_ref.shape[0]
    head = pl.program_id(0)

    @pl.when(head == 0)
    def _():
        fill_bias(starts_ref, bias_ref, rows)

    @pl.when(lax.rem(head, GROUP) == 0)
    def _():
        vt_ref[...] = v_ref[...].astype(jnp.float32).T.astype(jnp.bfloat16)

    for index, (at, low, high) in enumerate(windows(rows)):
        scores = dot(k_ref[low:high, :], q_ref[at : at + BLOCK, :], NT)
        scores = scores * (FACTOR * LOG2E) + bias_ref[index, 0 : high - low, :]
        top = jnp.max(scores, axis=0, keepdims=True)
        probs = jnp.exp2(scores - top)
        total = jnp.sum(probs, axis=0, keepdims=True)
        out = dot(vt_ref[:, low:high], probs.astype(jnp.bfloat16), NN)
        out_ref[at : at + BLOCK, :] = (out / total).T.astype(jnp.bfloat16)
        log_ref[0, 0:1, at : at + BLOCK] = top + jnp.log2(total)


def backward_kernel(
    starts_ref,
    q_ref,
    k_ref,
    v_ref,
    o_ref,
    g_ref,
    log_ref,
    dq_ref,
    dk_ref,
    dv_ref,
    bias_ref,
    kt_ref,
    dk_acc,
    dv_acc,
):
    rows = q_ref.shape[0]
    head = pl.program_id(0)

    @pl.when(head == 0)
    def _():
        fill_bias(starts_ref, bias_ref, rows)

    @pl.when(lax.rem(head, GROUP) == 0)
    def _():
        kt_ref[...] = k_ref[...].astype(jnp.float32).T.astype(jnp.bfloat16)
        dk_acc[...] = jnp.zeros_like(dk_acc)
        dv_acc[...] = jnp.zeros_like(dv_acc)

    for index, (at, low, high) in enumerate(windows(rows)):
        q = q_ref[at : at + BLOCK, :]
        g = g_ref[at : at + BLOCK, :]
        scores = dot(k_ref[low:high, :], q, NT)
        scores = scores * (FACTOR * LOG2E) + bias_ref[index, 0 : high - low, :]
        probs = jnp.exp2(scores - log_ref[0, 0:1, at : at + BLOCK])
        prob_grad = dot(v_ref[low:high, :], g, NT)
        product = g.astype(jnp.float32) * o_ref[at : at + BLOCK, :].astype(jnp.float32)
        delta = jnp.sum(product.T, axis=0, keepdims=True)
        score_grad = (probs * (prob_grad - delta)).astype(jnp.bfloat16)
        dv_acc[low:high, :] += dot(probs.astype(jnp.bfloat16), g, NN)
        dk_acc[low:high, :] += dot(score_grad, q, NN)
        dq = dot(kt_ref[:, low:high], score_grad, NN) * FACTOR
        dq_ref[at : at + BLOCK, :] = dq.T.astype(jnp.bfloat16)

    @pl.when(lax.rem(head, GROUP) == GROUP - 1)
    def _():
        dk_ref[...] = (dk_acc[...] * FACTOR).astype(jnp.bfloat16)
        dv_ref[...] = dv_acc[...].astype(jnp.bfloat16)


def attention_specs(rows):
    whole = pl.BlockSpec((1, rows), lambda h: (0, 0))
    one = pl.BlockSpec((rows, HEAD_SIZE), lambda h: (0, h))
    shared = pl.BlockSpec((rows, HEAD_SIZE), lambda h: (0, h // GROUP))
    logs = pl.BlockSpec((1, 1, rows), lambda h: (h, 0, 0))
    return whole, one, shared, logs


def attention_forward(starts, query, keys, values):
    rows, width = query.shape
    heads = width // HEAD_SIZE
    whole, one, shared, logs = attention_specs(rows)
    pairs = sum(high - low for _, low, high in windows(rows)) * BLOCK
    return pl.pallas_call(
        forward_kernel,
        grid=(heads,),
        in_specs=[whole, one, shared, shared],
        out_specs=[one, logs],
        out_shape=[
            jax.ShapeDtypeStruct((rows, width), jnp.bfloat16),
            jax.ShapeDtypeStruct((heads, 1, rows), jnp.float32),
        ],
        scratch_shapes=[
            pltpu.VMEM((rows // BLOCK, REACH + BLOCK, BLOCK), jnp.float32),
            pltpu.VMEM((HEAD_SIZE, rows), jnp.bfloat16),
        ],
        compiler_params=pltpu.CompilerParams(vmem_limit_bytes=40 * 1024 * 1024),
        cost_estimate=pl.CostEstimate(
            flops=heads * pairs * HEAD_SIZE * 2 * 2 * 3,
            bytes_accessed=rows * width * 2 * 3,
            transcendentals=heads * pairs,
        ),
        name="attention_forward",
    )(starts, query, keys, values)


def attention_backward(starts, query, keys, values, out, grad, logs_in):
    rows, width = query.shape
    heads = width // HEAD_SIZE
    whole, one, shared, logs = attention_specs(rows)
    pairs = sum(high - low for _, low, high in windows(rows)) * BLOCK
    return pl.pallas_call(
        backward_kernel,
        grid=(heads,),
        in_specs=[whole, one, shared, shared, one, one, logs],
        out_specs=[one, shared, shared],
        out_shape=[
            jax.ShapeDtypeStruct((rows, width), jnp.bfloat16),
            jax.ShapeDtypeStruct(keys.shape, jnp.bfloat16),
            jax.ShapeDtypeStruct(values.shape, jnp.bfloat16),
        ],
        scratch_shapes=[
            pltpu.VMEM((rows // BLOCK, REACH + BLOCK, BLOCK), jnp.float32),
            pltpu.VMEM((HEAD_SIZE, rows), jnp.bfloat16),
            pltpu.VMEM((rows, HEAD_SIZE), jnp.float32),
            pltpu.VMEM((rows, HEAD_SIZE), jnp.float32),
        ],
        compiler_params=pltpu.CompilerParams(vmem_limit_bytes=40 * 1024 * 1024),
        cost_estimate=pl.CostEstimate(
            flops=heads * pairs * HEAD_SIZE * 2 * 5 * 3,
            bytes_accessed=rows * width * 2 * 5,
            transcendentals=heads * pairs,
        ),
        name="attention_backward",
    )(starts, query, keys, values, out, grad, logs_in)


def shards(query, keys, values, out_weight, loss_grad, lengths, languages, labels):
    rows = query.shape[0]
    places = jnp.arange(rows, dtype=jnp.int32)
    order = jnp.arange(DOCS, dtype=jnp.int32)
    ends = jnp.sum(jnp.where(order[:, None] >= order[None, :], lengths[0][None, :], 0), axis=1)
    begins = ends - lengths[0]
    inside = (places[None, :] >= begins[:, None]) & (places[None, :] < ends[:, None])
    starts = jnp.sum(jnp.where(inside, begins[:, None], 0), axis=0)[None, :]
    full_grad = lax.all_gather(loss_grad, "tensor", axis=1, tiled=True)
    full_weight = lax.all_gather(out_weight, "dp", axis=1, tiled=True)
    token_lang = jnp.sum(jnp.where(inside, languages[0][:, None], 0), axis=0)
    counted = labels != -100
    lang_match = token_lang[:, None] == jnp.arange(LANGS, dtype=jnp.int32)[None, :]
    local_counts = jnp.sum((lang_match & counted[:, None]).astype(jnp.int32), axis=0)
    counts = lax.psum(local_counts, "dp").astype(jnp.float32)
    lang_weight = jnp.sqrt(jnp.sum(counts) / (LANGS * jnp.maximum(counts, 1.0)))
    token_weight = jnp.where(
        counted, jnp.sum(jnp.where(lang_match, lang_weight[None, :], 0.0), axis=1), 0.0
    )
    attention_result, logs = attention_forward(starts, query, keys, values)
    full_grad, full_weight = lax.optimization_barrier((full_grad, full_weight))
    weighted = (token_weight[:, None] * full_grad.astype(jnp.float32)).astype(jnp.bfloat16)
    local_term = dot(attention_result, weighted, TN).astype(jnp.bfloat16)
    own_rows = lax.psum_scatter(local_term, "dp", scatter_dimension=0, tiled=True)
    out_grad = dot(weighted, full_weight, NT).astype(jnp.bfloat16)
    own_rows, _ = lax.optimization_barrier((own_rows, out_grad))
    projection_gradient = lax.all_gather(own_rows, "dp", axis=0, tiled=True)
    query_gradient, key_gradient, value_gradient = attention_backward(
        starts, query, keys, values, attention_result, out_grad, logs
    )
    return (attention_result, query_gradient, key_gradient, value_gradient, projection_gradient)


def solution(mesh):
    in_specs = (
        P("dp", "tensor"),
        P("dp", "tensor"),
        P("dp", "tensor"),
        P("tensor", "dp"),
        P("dp", "tensor"),
        P("dp", None),
        P("dp", None),
        P("dp"),
    )
    out_specs = (
        P("dp", "tensor"),
        P("dp", "tensor"),
        P("dp", "tensor"),
        P("dp", "tensor"),
        P("tensor", None),
    )
    return jax.shard_map(shards, mesh=mesh, in_specs=in_specs, out_specs=out_specs, check_vma=False)
```

time: 612 us -> 294 us (0.48)
  blocking collectives: 271 us -> 9.47 us
  waiting for transfers between devices: 68.8 us -> 183 us
  matrix products: 102 us -> 24 us
  loops' own time: 63.1 us -> 0 us
  Pallas kernels: 0 us -> 43.5 us
  local copies, waits for them, and re-layouts: 57.8 us -> 14.5 us
  other arithmetic: 25.8 us -> 5.06 us
    psum x1 -> x0, blocking collectives: 259 us -> none  [shards(): projection_gradient = lax.psum(local_term, 'dp').astype(jnp.bfloat16)]
    dot_general x28 -> x2, matrix products: 102 us -> 24 us  [dot(): return lax.dot_general(a, b, dims, preferred_element_type=jnp.float32)]
    reduce_scatter x0 -> x1, waiting for transfers between devices: none -> 50.9 us  [shards(): lax.psum_scatter(local_term, 'dp', scatter_dimension=0, tiled=True)]
    pallas_call x0 -> x2, Pallas kernels: none -> 43.5 us  [the longest x1 22 us: attention_forward(): pl.pallas_call(forward_kernel, grid=(heads,), in_specs=[whole, one, share...]
    all_gather x1, waiting for transfers between devices: 20.5 us -> 61.2 us  [shards(): full_grad = lax.all_gather(loss_grad, 'tensor', axis=1, tiled=True)]
    another operation x2 -> x0, loops' own time: 37.1 us -> none  [pack_backward(): lax.switch(bucket, [later_block(bucket_id) for bucket_id in range(5)], (q...]
    unnamed x2 -> x0, loops' own time: 26.1 us -> none
    all_gather x1 -> x2, waiting for transfers between devices: 46.9 us -> 69.4 us  [the longest x1 46.9 us: shards(): full_weight = lax.all_gather(out_weight, 'dp', axis=1, tiled=True)]
  transfers between devices with their start and end apart: 2 -> 4, of which waited for: 2 -> 4; matrix products, arithmetic and copies ran while one was open for 6% -> 6% of each run, Pallas kernels for 0% -> 15%
where the time goes in v1:
time: 294 us; the launch traced here: 293 us
  waiting for transfers between devices  183 us (62%)
  Pallas kernels  43.5 us (15%)
  matrix products  24 us (8%)
  local copies, waits for them, and re-layouts  14.5 us (5%)
  between operations  13.8 us (5%)
  blocking collectives  9.47 us (3%)
  other arithmetic  5.06 us (2%)
    all_gather x1, waiting for transfers between devices, shards(): full_grad = lax.all_gather(loss_grad, 'tensor', axis=1, tiled=True)  61.2 us
    reduce_scatter x1, waiting for transfers between devices, shards(): lax.psum_scatter(local_term, 'dp', scatter_dimension=0, tiled=True)  50.9 us
    all_gather x1, waiting for transfers between devices, shards(): full_weight = lax.all_gather(out_weight, 'dp', axis=1, tiled=True)  46.9 us
    dot_general x2, matrix products, dot(): return lax.dot_general(a, b, dims, preferred_element_type=jnp.float32)  24 us
    all_gather x1, waiting for transfers between devices, shards(): projection_gradient = lax.all_gather(own_rows, 'dp', axis=0, tiled=True)  22.5 us
    pallas_call x1, Pallas kernels, attention_forward(): pl.pallas_call(forward_kernel, grid=(heads,), in_specs=[whole, one, share...  22 us
    pallas_call x1, Pallas kernels, attention_backward(): pl.pallas_call(backward_kernel, grid=(heads,), in_specs=[whole, one, shar...  21.5 us
    unnamed x17, local copies, waits for them, and re-layouts  14.5 us
  transfers between devices with their start and end apart: 4, of which 4 were waited for; matrix products, arithmetic and copies ran while one was open for 6% of the time, Pallas kernels for 15%

profile of v1, /device:TPU:0, one launch (start us, length us, event | category | flops | bytes accessed | tf_op | source)
XLA Modules:
  0.0 293.4 jit_solution(3966728222638712001)
XLA Ops:
  7.2 0.0 all-gather.4.cloned.1.call-start
  7.2 0.7 all-gather.4.cloned.1.call-update
  7.9 0.0 all-gather.6.cloned.1.call-start
  7.9 0.7 all-gather.6.cloned.1.call-update
  8.6 0.0 reduce-scatter.2.cloned.1.call-start
  8.7 0.8 select_reduce_fusion.3
  9.5 0.7 bitcast_subtract_fusion
  10.1 0.8 select_reduce_fusion.1
  10.9 0.7 broadcast_compare_fusion
  11.6 0.1 convert_reduce_fusion
  11.7 9.5 %psum.7 = s32[29]{0:T(128)S(1)} all-reduce(s32[29]{0:T(128)S(1)} %convert_reduce_fusion), channel_id=1, replica_groups=mesh['dp'=8,'tensor'=4] {'dp'}, use_global_device_ids=true, to_apply=%region_4.5 | all-reduce | flops 29 | bytes 232 | tf_op jit(solution)/shard_map/psum | solution.py:196
  21.2 0.6 convert_reduce_fusion.1
  21.8 0.7 divide_sqrt_fusion
  22.4 0.1 select_reduce_fusion
  22.6 0.7 broadcast_select_fusion
  23.3 1.8 copy-done
  25.0 1.0 copy-done.2
  26.1 1.0 copy-done.4
  27.1 22.0 %attention_forward.1 = (bf16[1024,1280]{1,0:T(8,128)(2,1)}, f32[10,1,1024]{2,1,0:T(1,128)S(1)}) custom-call(s32[1,1024]{1,0:T(1,128)S(1)} %bitcast.6, bf16[1024,1280]{1,0:T(8,128)(2,1)S(1)} %copy-done, bf16[1024,256]{1,0:T(8,128)(2,1)S(1)} %copy-done.2, bf16[1024,256]{1,0:T(8,128)(2,1)S(1)} %copy-done.4), custom_call_target="tpu_custom_call" | custom-call | flops 9059696640 | bytes 7864320 | tf_op jit(solution)/shard_map/attention_forward/pallas_call | solution.py:128
  49.2 61.2 %all-gather.4.cloned.1.call-done = bf16[1024,2560]{1,0:T(8,128)(2,1)} async-done(((bf16[1024,640]{1,0:T(8,128)(2,1)}), bf16[1024,2560]{1,0:T(8,128)(2,1)}) %all-gather.4.cloned.1.call-update) | async-done | bytes 5242896 | tf_op jit(solution)/shard_map/all_gather | solution.py:190
  110.4 46.9 %all-gather.6.cloned.1.call-done = bf16[1280,2560]{0,1:T(8,128)(2,1)} async-done(((bf16[1280,320]{0,1:T(8,128)(2,1)}), bf16[1280,2560]{0,1:T(8,128)(2,1)}) %all-gather.6.cloned.1.call-update) | async-done | bytes 6553616 | tf_op jit(solution)/shard_map/all_gather | solution.py:191
  157.3 11.8 %convolution_convert_fusion = bf16[1280,2560]{1,0:T(8,128)(2,1)} fusion(bf16[1024,1280]{1,0:T(8,128)(2,1)} %get-tuple-element.28.o_ref, bf16[1024,2560]{1,0:T(8,128)(2,1)} %all-gather.4.cloned.1.call-done, f32[1024]{0:T(1024)S(1)} %broadcast_select_fusion), kind=kOutput, calls=%fused_computation | convolution fusion | flops 6722027520 | bytes 14422016 | tf_op jit(solution)/shard_map/dot_general | solution.py:26
  169.1 0.0 reduce-scatter.2.cloned.1.call-update
  169.2 0.0 all-gather.8.cloned.1.call-start
  169.2 12.2 %convolution_convert_fusion.1.g_ref = bf16[1024,1280]{1,0:T(8,128)(2,1)} fusion(bf16[1280,2560]{0,1:T(8,128)(2,1)} %all-gather.6.cloned.1.call-done, bf16[1024,2560]{1,0:T(8,128)(2,1)} %all-gather.4.cloned.1.call-done, f32[1024]{0:T(1024)S(1)} %broadcast_select_fusion), kind=kOutput, calls=%fused_computation.2 | convolution fusion | flops 6720061440 | bytes 14422016 | tf_op jit(solution)/shard_map/dot_general | solution.py:26
  181.4 50.9 %reduce-scatter.2.cloned.1.call-done = bf16[160,2560]{1,0:T(8,128)(2,1)} async-done(((bf16[1280,2560]{1,0:T(8,128)(2,1)}), bf16[160,2560]{1,0:T(8,128)(2,1)}) %reduce-scatter.2.cloned.1.call-update) | async-done | bytes 819216 | tf_op jit(solution)/shard_map/reduce_scatter | solution.py:205
  232.3 1.0 copy-done.5
  233.4 1.7 copy-done.6
  235.1 1.7 copy-done.7
  236.9 21.5 %attention_backward.1 = (bf16[1024,1280]{1,0:T(8,128)(2,1)}, bf16[1024,256]{1,0:T(8,128)(2,1)}, bf16[1024,256]{1,0:T(8,128)(2,1)}) custom-call(s32[1,1024]{1,0:T(1,128)S(1)} %bitcast.7, bf16[1024,1280]{1,0:T(8,128)(2,1)S(1)} %copy-done.1, bf16[1024,256]{1,0:T(8,128)(2,1)S(1)} %copy-done.3, bf16[1024,256]{1,0:T(8,128)(2,1)S(1)} %copy-done.5, ...), custom_call_target="tpu_custom_call" | custom-call | flops 22649241600 | bytes 13107200 | tf_op jit(solution)/shard_map/attention_backward/pallas_call | solution.py:156
  258.3 22.5 %all-gather.8.cloned.1.call-done = bf16[1280,2560]{1,0:T(8,128)(2,1)} async-done(((bf16[160,2560]{1,0:T(8,128)(2,1)}), bf16[1280,2560]{1,0:T(8,128)(2,1)}) %all-gather.8.cloned.1.call-update) | async-done | bytes 6553616 | tf_op jit(solution)/shard_map/all_gather | solution.py:208
  280.8 6.1 %copy.14 = bf16[1280,2560]{1,0:T(8,128)(2,1)} copy(bf16[1280,2560]{1,0:T(8,128)(2,1)} %all-gather.8.cloned.1.call-done) | data formatting | bytes 13107200
  (11 shorter events, 0.0 us)
Async XLA Ops:
  7.2 103.2 %all-gather.4.cloned.1.call-start = ((), (), s32[]{:S(2)}) async-start(), calls=%async_computation.1 | async-start | bytes 6553600 | tf_op jit(solution)/shard_map/all_gather | solution.py:190
  7.9 149.4 %all-gather.6.cloned.1.call-start = ((), (), s32[]{:S(2)}) async-start(), calls=%async_computation.2 | async-start | bytes 7372800 | tf_op jit(solution)/shard_map/all_gather | solution.py:191
  8.6 223.6 %reduce-scatter.2.cloned.1.call-start = ((), (), s32[]{:S(2)}) async-start(), calls=%async_computation.3 | async-start | bytes 7372800 | tf_op jit(solution)/shard_map/reduce_scatter | solution.py:205
  23.2 1.8 copy-start
  25.0 1.0 copy-start.2
  26.1 1.0 copy-start.4
  169.1 63.2 %copy-start.1 = (bf16[1024,1280]{1,0:T(8,128)(2,1)S(1)}, bf16[1024,1280]{1,0:T(8,128)(2,1)}, u32[]{:S(2)}) copy-start(bf16[1024,1280]{1,0:T(8,128)(2,1)} %q_ref.3) | copy-start | bytes 7864324
  169.2 63.2 %copy-start.3 = (bf16[1024,256]{1,0:T(8,128)(2,1)S(1)}, bf16[1024,256]{1,0:T(8,128)(2,1)}, u32[]{:S(2)}) copy-start(bf16[1024,256]{1,0:T(8,128)(2,1)} %k_ref.3) | copy-start | bytes 1572868
  169.2 111.7 %all-gather.8.cloned.1.call-start = ((), (), s32[]{:S(2)}) async-start(), calls=%async_computation.4 | async-start | bytes 7372800 | tf_op jit(solution)/shard_map/all_gather | solution.py:208
  232.3 1.0 copy-start.5
  233.4 1.7 copy-start.6
  235.1 1.7 copy-start.7
Sparse Core Ops, SparseCore 0:
  9.6 100.7 all-gather.3
  112.3 44.9 all-gather.5
  169.3 62.9 reduce-scatter.1
  234.2 46.6 all-gather.7
